TPU v7x, 32 devices: a whole 2x2x4 slice. The times are simulated.
32 devices in a mesh: tm: 4 (over z), owner: 8 (over y, x, core).
Axes of the slice: x: 2, y: 2, z: 4, core: 2. Of those that a mesh axis runs over, the one named last changes fastest.
Arguments:
- pressure: bfloat16 [512, 32768], P('tm', 'owner'), may hold values from -6 to 6
- proj_weight: bfloat16 [8, 32, 4, 128, 128], P('owner', 'tm'), may hold values from -0.25 to 0.25
- pattern: int32 [8, 32, 4], P('owner', 'tm'), may hold values from 0 to 31, as said below
- panel_list: int32 [8, 32], replicated, may hold values from 0 to 191, as said below
- owner_list: int32 [8, 36], replicated, may hold values from -1 to 191, as said below
- owner_count: int32 [8], replicated, may hold values from 12 to 36, as said below
Outputs:
- panel_field: float32 [288, 512, 128], P('owner', 'tm')
Inputs may be any that keep to these rules, and one draw needn't show every extreme that they name: `pattern`: the 4 entries of one face block are different. `panel_list`: each row names different panel blocks, owned by 8 different owners, exactly 4 of each. `owner_list`: slots below an owner's count hold its panel blocks; every panel block stands in exactly one such slot; slots from the count on hold -1. `owner_count`: the counts sum to 192.
All inputs are finite; a program needn't handle non-finite values.
Results may differ from a plain program's by a relative error of at most 0.0003.
Values may be sent and summed in bfloat16 or wider, within the bound.
A program may use at most 128 MiB of HBM per device.

v0:
```python
import jax
import jax.numpy as jnp
from jax import lax
from jax.sharding import PartitionSpec as P


def routing_tables(panel_list, owner_list, owner_count, slot_count):
    owner_size, list_len = panel_list.shape
    capacity = owner_list.shape[1]
    owners = jnp.arange(owner_size, dtype=jnp.int32)
    owned_slots = jnp.arange(capacity, dtype=jnp.int32)[None, :] < owner_count[:, None]
    matches = (panel_list[:, :, None, None] == owner_list[None, None, :, :]) & owned_slots[
        None, None, :, :
    ]
    target = jnp.sum(jnp.where(matches, owners[None, None, :, None], 0), axis=(2, 3))
    position = jnp.arange(list_len, dtype=jnp.int32)
    earlier = (target[:, :, None] == target[:, None, :]) & (
        position[None, None, :] < position[None, :, None]
    )
    order_rank = jnp.sum(earlier.astype(jnp.int32), axis=2)
    slot_ids = jnp.arange(slot_count, dtype=jnp.int32)
    placed = (target[:, :, None, None] == owners[None, None, :, None]) & (
        order_rank[:, :, None, None] == slot_ids[None, None, None, :]
    )
    filled = jnp.sum(placed.astype(jnp.int32), axis=1)
    source_row = jnp.sum(jnp.where(placed, position[None, :, None, None], 0), axis=1) + list_len * (
        1 - filled
    )
    carried = jnp.sum(jnp.where(placed, panel_list[:, :, None, None], 0), axis=1) - (1 - filled)
    return (source_row, carried)


def pack_rows(values, outgoing, owner_size, slot_count):
    padded = jnp.concatenate([values, jnp.zeros((1,) + values.shape[1:], jnp.float32)], axis=0)
    packed = jnp.take(padded, outgoing, axis=0)
    return packed.reshape((owner_size, slot_count) + values.shape[1:])


def collect(received, slot_panels, owner_list, owner_count, own_index):
    capacity = owner_list.shape[1]
    wanted = owner_list[own_index]
    live_count = owner_count[own_index]
    slot_ids = jnp.arange(capacity, dtype=jnp.int32)
    live_slots = slot_ids < live_count
    incoming = slot_panels.reshape(-1)
    match = (incoming[:, None] == wanted[None, :]) & live_slots[None, :]
    found = jnp.sum(match.astype(jnp.int32), axis=1)
    dest = jnp.sum(jnp.where(match, slot_ids[None, :], 0), axis=1) + capacity * (1 - found)
    flat_rows = received.reshape((incoming.shape[0],) + received.shape[2:])
    combined = jax.ops.segment_sum(flat_rows, dest, num_segments=capacity + 1)
    return combined[:capacity]


def body(pressure, proj_weight, pattern, panel_list, owner_list, owner_count):
    owner_size = lax.axis_size("owner")
    own_index = lax.axis_index("owner")
    series = lax.all_to_all(pressure, "tm", split_axis=1, concat_axis=0, tiled=True)
    time_len = series.shape[0]
    fb_dev = pattern.shape[1]
    block_len = proj_weight.shape[-1]
    list_len = panel_list.shape[1]
    slot_count = max(2, list_len // owner_size)
    series = series.reshape(time_len, fb_dev, block_len)
    contrib = jnp.einsum(
        "tia,ikab->iktb", series, proj_weight[0], preferred_element_type=jnp.float32
    )
    flat_contrib = contrib.reshape((-1, time_len, block_len))
    partial_value = (
        jnp.zeros((list_len, time_len, block_len), jnp.float32)
        .at[pattern[0].reshape(-1)]
        .add(flat_contrib)
    )
    source_row, carried = routing_tables(panel_list, owner_list, owner_count, slot_count)
    outgoing = jnp.take(source_row, own_index, axis=0).reshape(-1)
    slot_panels = jnp.take(carried, own_index, axis=1)
    packed = pack_rows(partial_value, outgoing, owner_size, slot_count)
    received = lax.all_to_all(packed, "owner", split_axis=0, concat_axis=0, tiled=True)
    combined = collect(received, slot_panels, owner_list, owner_count, own_index)
    return lax.psum_scatter(combined, "tm", scatter_dimension=1, tiled=True)


def solution(mesh):
    placed = (
        P("tm", "owner"),
        P("owner", "tm", None, None, None),
        P("owner", "tm", None),
        P(),
        P(),
        P(),
    )
    return jax.shard_map(
        body, mesh=mesh, in_specs=placed, out_specs=P("owner", "tm", None), check_vma=False
    )
```

profile of v0, /device:TPU:1, one launch (start us, length us, event | category | flops | bytes accessed | tf_op | source)
XLA Modules:
  0.0 396.7 jit_solution(8157800736488065897)
XLA Ops:
  6.5 2.4 copy.34
  8.9 5.4 %all-to-all-start = ((bf16[128,4,1024]{2,0,1:T(8,128)(2,1)}), bf16[128,4,1024]{2,0,1:T(8,128)(2,1)S(1)}, u32[]{:S(2)}, u32[]{:S(2)}) async-start(bf16[128,4,1024]{2,0,1:T(8,128)(2,1)} %bitcast.28), calls=%async_computation | async-start | bytes 2097152 | tf_op jit(solution)/shard_map/all_to_all | solution.py:57
  14.3 0.7 iota_compare_fusion.3
  15.1 0.8 copy.19
  15.8 0.1 reshape_squeeze.3
  15.9 5.6 %select_reduce_fusion = s32[8,32]{1,0:T(8,128)S(1)} fusion(s32[8,36]{1,0:T(8,128)} %param.10, s32[8,32]{1,0:T(8,128)} %param.9, pred[8,36]{1,0:T(8,128)(4,1)S(1)} %iota_compare_fusion.3), kind=kLoop, calls=%fused_computation.8 | loop fusion | flops 294656 | bytes 3488 | tf_op jit(solution)/shard_map/reduce_sum | solution.py:15
  21.5 0.3 convert_reduce_fusion
  21.9 2.4 fusion.5
  24.3 0.1 copy.18
  24.4 0.1 copy.24
  24.5 0.1 select_n.96
  24.6 15.0 %all-to-all-done = bf16[128,4,1024]{2,0,1:T(8,128)(2,1)S(1)} async-done(((bf16[128,4,1024]{2,0,1:T(8,128)(2,1)}), bf16[128,4,1024]{2,0,1:T(8,128)(2,1)S(1)}, u32[]{:S(2)}, u32[]{:S(2)}) %all-to-all-start) | async-done | bytes 1048608 | tf_op jit(solution)/shard_map/all_to_all | solution.py:57
  39.6 0.3 copy.30
  39.8 4.5 %fusion = f32[8,4,128,512]{3,2,1,0:T(8,128)} fusion(bf16[512,8,128,1]{2,1,0,3:T(8,128)(2,1)S(1)} %bitcast.31, bf16[1,8,4,128,128]{4,3,2,1,0:T(8,128)(2,1)S(1)} %copy-done), kind=kOutput, calls=%fused_computation.5 | convolution fusion | flops 536870912 | bytes 10485760 | tf_op jit(solution)/shard_map/tia,ikab->iktb/dot_general | solution.py:64
  44.4 9.0 %copy.23 = f32[32,512,128]{2,1,0:T(8,128)} copy(f32[32,512,128]{1,2,0:T(8,128)} %bitcast.29) | data formatting | bytes 16777216 | tf_op jit(solution)/shard_map/reshape | solution.py:67
  53.3 4.2 %broadcast_in_dim.113 = f32[32,512,128]{2,1,0:T(8,128)} broadcast(f32[]{:T(128)} %constant.25.clone.1), dimensions={} | broadcast | bytes 8388612 | tf_op jit(solution)/shard_map/broadcast_in_dim | solution.py:69
  57.5 18.8 %scatter_fusion = f32[32,512,128]{2,1,0:T(8,128)} fusion(f32[32,512,128]{2,1,0:T(8,128)} %broadcast_in_dim.113, s32[32]{0:T(128)S(1)} %get-tuple-element.34, f32[32,512,128]{2,1,0:T(8,128)} %copy.23), kind=kCustom, calls=%fused_computation.1 | custom fusion | flops 2097152 | bytes 25165952 | tf_op jit(solution)/shard_map/scatter-add | solution.py:71
  76.4 7.7 %concatenate.3 = f32[33,512,128]{2,1,0:T(8,128)} pad(f32[32,512,128]{2,1,0:T(8,128)} %scatter_fusion, f32[]{:T(128)} %constant.25.clone.1), padding=0_1x0_0x0_0 | pad | bytes 17039364 | tf_op jit(solution)/shard_map/concatenate | solution.py:34
  84.0 7.8 %gather_fusion = f32[32,512,128]{2,1,0:T(8,128)} fusion(f32[33,512,128]{2,1,0:T(8,128)} %concatenate.3, s32[1024]{0:T(1024)S(1)} %pad_clamp_fusion), kind=kCustom, calls=%fused_computation | custom fusion | bytes 16777344 | tf_op jit(solution)/shard_map/jit(_take)/gather | solution.py:35
  91.8 7.8 %broadcast_select_fusion = f32[8,4,512,128]{3,2,1,0:T(8,128)} fusion(f32[8,4,512,128]{3,2,1,0:T(8,128)} %bitcast.30, pred[8,4]{1,0:T(8,128)(4,1)S(1)} %copy.18), kind=kLoop, calls=%fused_computation.3 | loop fusion | flops 2097152 | bytes 16777248 | tf_op jit(solution)/shard_map/jit(_take)/select_n | solution.py:35
  99.6 6.4 %all-to-all-start.1 = ((f32[8,4,512,128]{3,2,1,0:T(8,128)}), f32[8,4,512,128]{3,2,1,0:T(8,128)}, u32[]{:S(2)}, u32[]{:S(2)}) async-start(f32[8,4,512,128]{3,2,1,0:T(8,128)} %broadcast_select_fusion), calls=%async_computation.1 | async-start | bytes 16777216 | tf_op jit(solution)/shard_map/all_to_all | solution.py:77
  106.1 0.6 dynamic_slice.7
  106.6 0.3 fusion.7
  106.9 0.1 select_n.90
  107.0 0.7 fusion.9
  107.7 0.6 iota_compare_fusion.4
  108.4 0.2 convert_reduce_fusion.1
  108.6 88.0 %all-to-all-done.1 = f32[8,4,512,128]{3,2,1,0:T(8,128)} async-done(((f32[8,4,512,128]{3,2,1,0:T(8,128)}), f32[8,4,512,128]{3,2,1,0:T(8,128)}, u32[]{:S(2)}, u32[]{:S(2)}) %all-to-all-start.1) | async-done | bytes 8388640 | tf_op jit(solution)/shard_map/all_to_all | solution.py:77
  196.6 4.9 %broadcast_in_dim.101 = f32[37,512,128]{2,1,0:T(8,128)} broadcast(f32[]{:T(128)} %constant.25.clone.1), dimensions={} | broadcast | bytes 9699332 | tf_op jit(solution)/shard_map/broadcast_in_dim | solution.py:50
  201.5 18.9 %scatter_fusion.1 = f32[37,512,128]{2,1,0:T(8,128)} fusion(f32[37,512,128]{2,1,0:T(8,128)} %broadcast_in_dim.101, s32[32]{0:T(128)S(1)} %multiply_add_fusion, f32[32,512,128]{2,1,0:T(8,128)} %bitcast.11), kind=kCustom, calls=%fused_computation.2 | custom fusion | flops 2097152 | bytes 25165952 | tf_op jit(solution)/shard_map/scatter-add | solution.py:50
  220.4 8.4 %slice.24 = f32[36,512,128]{2,1,0:T(8,128)} slice(f32[37,512,128]{2,1,0:T(8,128)} %scatter_fusion.1), slice={[0:36], [0:512], [0:128]} | slice | bytes 18874368 | tf_op jit(solution)/shard_map/slice | solution.py:51
  228.8 161.1 %reduce-scatter.2.cloned.1.call-done = f32[36,128,128]{2,1,0:T(8,128)} async-done(((f32[36,512,128]{2,1,0:T(8,128)}), f32[36,128,128]{2,1,0:T(8,128)}) %reduce-scatter.2.cloned.1.call-update) | async-done | bytes 2359312 | tf_op jit(solution)/shard_map/reduce_scatter | solution.py:79
  (16 shorter events, 0.1 us)
Async XLA Ops:
  6.5 33.3 %copy-start = (bf16[1,8,4,128,128]{4,3,2,1,0:T(8,128)(2,1)S(1)}, bf16[1,8,4,128,128]{4,3,2,1,0:T(8,128)(2,1)}, u32[]{:S(2)}) copy-start(bf16[1,8,4,128,128]{4,3,2,1,0:T(8,128)(2,1)} %param.7) | copy-start | bytes 3145732
  8.9 30.7 %all-to-all-start = ((bf16[128,4,1024]{2,0,1:T(8,128)(2,1)}), bf16[128,4,1024]{2,0,1:T(8,128)(2,1)S(1)}, u32[]{:S(2)}, u32[]{:S(2)}) async-start(bf16[128,4,1024]{2,0,1:T(8,128)(2,1)} %bitcast.28), calls=%async_computation | async-start | bytes 2097152 | tf_op jit(solution)/shard_map/all_to_all | solution.py:57
  99.6 6.5 %copy-start.2 = (s32[8]{0:T(128)S(1)}, s32[8]{0:T(128)}, u32[]{:S(2)}) copy-start(s32[8]{0:T(128)} %param.11) | copy-start | bytes 100
  99.6 97.0 %all-to-all-start.1 = ((f32[8,4,512,128]{3,2,1,0:T(8,128)}), f32[8,4,512,128]{3,2,1,0:T(8,128)}, u32[]{:S(2)}, u32[]{:S(2)}) async-start(f32[8,4,512,128]{3,2,1,0:T(8,128)} %broadcast_select_fusion), calls=%async_computation.1 | async-start | bytes 16777216 | tf_op jit(solution)/shard_map/all_to_all | solution.py:77
  106.0 283.8 %reduce-scatter.2.cloned.1.call-start = ((), (), s32[]{:S(2)}) async-start(), calls=%async_computation.3 | async-start | bytes 11796480 | tf_op jit(solution)/shard_map/reduce_scatter | solution.py:79
  220.3 169.5 %copy-start.1 = (bf16[1,8,4,128,128]{4,3,2,1,0:T(8,128)(2,1)S(1)}, bf16[1,8,4,128,128]{4,3,2,1,0:T(8,128)(2,1)}, u32[]{:S(2)}) copy-start(bf16[1,8,4,128,128]{4,3,2,1,0:T(8,128)(2,1)} %param.7) | copy-start | bytes 3145732
Sparse Core Ops, SparseCore 0:
  228.9 160.9 reduce-scatter.1
where the time goes:
time: 398 us; the launch traced here: 397 us
  waiting for transfers between devices  264 us (66%)
  other arithmetic  55.7 us (14%)
  local copies, waits for them, and re-layouts  47 us (12%)
  between operations  13.5 us (3%)
  starting transfers between devices  11.9 us (3%)
  matrix products  4.51 us (1%)
    reduce_scatter x1, waiting for transfers between devices, body(): return lax.psum_scatter(combined, 'tm', scatter_dimension=1, tiled=True)  161 us
    all_to_all x1, waiting for transfers between devices, body(): lax.all_to_all(packed, 'owner', split_axis=0, concat_axis=0, tiled=True)  88 us
    scatter-add x1, other arithmetic, collect(): combined = jax.ops.segment_sum(flat_rows, dest, num_segments=capacity + 1)  18.9 us
    scatter-add x1, other arithmetic, body(): partial_value = jnp.zeros((list_len, time_len, block_len), jnp.float32).a...  18.8 us
    all_to_all x1, waiting for transfers between devices, body(): lax.all_to_all(pressure, 'tm', split_axis=1, concat_axis=0, tiled=True)  15 us
    reshape x1, local copies, waits for them, and re-layouts, body(): flat_contrib = contrib.reshape((-1, time_len, block_len))  8.95 us
    slice x1, local copies, waits for them, and re-layouts, collect(): return combined[:capacity]  8.43 us
  transfers between devices with their start and end apart: 3, of which 3 were waited for; matrix products, arithmetic and copies ran while one was open for 3% of the time, Pallas kernels for 0%

commit v1 on v0

v1 whole, which is shorter than its diff:
```python
import functools

import jax
import jax.numpy as jnp
from jax import lax
from jax.experimental import pallas as pl
from jax.experimental.pallas import tpu as pltpu
from jax.sharding import PartitionSpec as P

MESH = pl.DeviceIdType.MESH
PIECES = 4


def gather_kernel(n, w_ref, pat_ref, wg_ref, pg_ref, own_sem, send_sem, recv_sem, psend, precv):
    m = lax.axis_index("tm")
    per = w_ref.shape[0] // PIECES

    barrier = pltpu.get_barrier_semaphore()
    for step in range(1, n):
        pl.semaphore_signal(
            barrier, inc=1, device_id={"tm": lax.rem(m + step, n)}, device_id_type=MESH
        )
    pl.semaphore_wait(barrier, n - 1)

    def part(q):
        return pl.ds(q * per, per)

    own = pltpu.make_async_copy(w_ref, wg_ref.at[m], own_sem.at[0])
    own.start()
    own_pat = pltpu.make_async_copy(pat_ref, pg_ref.at[m], own_sem.at[1])
    own_pat.start()

    def send(way, hop, q):
        toward = m + 1 if way == 0 else m - 1
        origin = m - hop if way == 0 else m + hop
        origin = jnp.clip(origin, 0, n - 1)
        source = w_ref.at[part(q)] if hop == 0 else wg_ref.at[origin, part(q)]
        return pltpu.make_async_remote_copy(
            src_ref=source,
            dst_ref=wg_ref.at[origin, part(q)],
            send_sem=send_sem.at[way, hop, q],
            recv_sem=recv_sem.at[way, hop, q],
            device_id={"tm": jnp.clip(toward, 0, n - 1)},
            device_id_type=MESH,
        )

    def landed(way, hop, q):
        origin = m - 1 - hop if way == 0 else m + 1 + hop
        origin = jnp.clip(origin, 0, n - 1)
        return pltpu.make_async_remote_copy(
            src_ref=w_ref.at[part(q)],
            dst_ref=wg_ref.at[origin, part(q)],
            send_sem=send_sem.at[way, hop, q],
            recv_sem=recv_sem.at[way, hop, q],
            device_id={"tm": lax.rem(m + 1, n)},
            device_id_type=MESH,
        )

    def sends(way, hop):
        return (m - hop >= 0) & (m + 1 < n) if way == 0 else (m + hop < n) & (m >= 1)

    def lands(way, hop):
        return m - 1 - hop >= 0 if way == 0 else m + 1 + hop < n

    for q in range(PIECES):
        for way in range(2):
            @pl.when(sends(way, 0))
            def _():
                send(way, 0, q).start()

    def pat_copy(step):
        return pltpu.make_async_remote_copy(
            src_ref=pat_ref,
            dst_ref=pg_ref.at[m],
            send_sem=psend.at[step],
            recv_sem=precv.at[step],
            device_id={"tm": lax.rem(m + step, n)},
            device_id_type=MESH,
        )

    def pat_landed(step):
        return pltpu.make_async_remote_copy(
            src_ref=pat_ref,
            dst_ref=pg_ref.at[lax.rem(m - step + n, n)],
            send_sem=psend.at[step],
            recv_sem=precv.at[step],
            device_id={"tm": lax.rem(m + step, n)},
            device_id_type=MESH,
        )

    for step in range(1, n):
        pat_copy(step).start()

    for hop in range(n - 1):
        for q in range(PIECES):
            for way in range(2):
                @pl.when(lands(way, hop))
                def _():
                    landed(way, hop, q).wait_recv()
                if hop + 1 < n - 1:
                    @pl.when(sends(way, hop + 1))
                    def _():
                        send(way, hop + 1, q).start()
    for hop in range(n - 1):
        for q in range(PIECES):
            for way in range(2):
                @pl.when(sends(way, hop))
                def _():
                    send(way, hop, q).wait_send()
    for step in range(1, n):
        pat_landed(step).wait_recv()
        pat_copy(step).wait_send()
    own.wait()
    own_pat.wait()


def gather(weights, pattern, n):
    any_space = pl.BlockSpec(memory_space=pl.ANY)
    return pl.pallas_call(
        functools.partial(gather_kernel, n),
        out_shape=(
            jax.ShapeDtypeStruct((n,) + weights.shape, weights.dtype),
            jax.ShapeDtypeStruct((n,) + pattern.shape, pattern.dtype),
        ),
        in_specs=[any_space] * 2,
        out_specs=(any_space, any_space),
        scratch_shapes=[
            pltpu.SemaphoreType.DMA((2,)),
            pltpu.SemaphoreType.DMA((2, n - 1, PIECES)),
            pltpu.SemaphoreType.DMA((2, n - 1, PIECES)),
            pltpu.SemaphoreType.DMA((n,)),
            pltpu.SemaphoreType.DMA((n,)),
        ],
        compiler_params=pltpu.CompilerParams(collective_id=0, has_side_effects=True),
        name="gather_weights",
    )(weights, pattern)


def exchange_kernel(n, in_ref, out_ref, own_sem, send_sem, recv_sem):
    me = lax.axis_index("owner")
    barrier = pltpu.get_barrier_semaphore()
    for step in range(1, n):
        pl.semaphore_signal(
            barrier, inc=1, device_id={"owner": lax.rem(me + step, n)}, device_id_type=MESH
        )
    pl.semaphore_wait(barrier, n - 1)

    def copy(step, landing):
        peer = lax.rem(me + step, n)
        return pltpu.make_async_remote_copy(
            src_ref=in_ref.at[peer],
            dst_ref=out_ref.at[landing],
            send_sem=send_sem.at[step],
            recv_sem=recv_sem.at[step],
            device_id={"owner": peer},
            device_id_type=MESH,
        )

    for step in range(1, n):
        copy(step, me).start()
    own = pltpu.make_async_copy(in_ref.at[me], out_ref.at[me], own_sem)
    own.start()
    for step in range(1, n):
        copy(step, lax.rem(me - step + n, n)).wait_recv()
        copy(step, me).wait_send()
    own.wait()


def exchange(packed, n):
    any_space = pl.BlockSpec(memory_space=pl.ANY)
    return pl.pallas_call(
        functools.partial(exchange_kernel, n),
        out_shape=jax.ShapeDtypeStruct(packed.shape, packed.dtype),
        in_specs=[any_space],
        out_specs=any_space,
        scratch_shapes=[
            pltpu.SemaphoreType.DMA,
            pltpu.SemaphoreType.DMA((n,)),
            pltpu.SemaphoreType.DMA((n,)),
        ],
        compiler_params=pltpu.CompilerParams(collective_id=1, has_side_effects=True),
        name="exchange_sums",
    )(packed)


def product_kernel(fb, kp, rows_ref, p_ref, w_ref, out_ref):
    g = pl.program_id(0)

    @pl.when(g == 0)
    def _():
        out_ref[...] = jnp.zeros_like(out_ref)

    block = w_ref.shape[-1]
    for i in range(fb):
        x = p_ref[:, i * block : (i + 1) * block]
        for k in range(kp):
            row = rows_ref[(g * fb + i) * kp + k]
            out_ref[row] += jnp.dot(x, w_ref[0, i, k], preferred_element_type=jnp.float32)


def products(rows, pressure, gathered, list_len):
    n, fb, kp, block, _ = gathered.shape
    time_len = pressure.shape[0]
    return pl.pallas_call(
        functools.partial(product_kernel, fb, kp),
        out_shape=jax.ShapeDtypeStruct((list_len, time_len, block), jnp.float32),
        grid_spec=pltpu.PrefetchScalarGridSpec(
            num_scalar_prefetch=1,
            grid=(n,),
            in_specs=[
                pl.BlockSpec((time_len, fb * block), lambda g, rows: (0, g)),
                pl.BlockSpec((1, fb, kp, block, block), lambda g, rows: (g, 0, 0, 0, 0)),
            ],
            out_specs=pl.BlockSpec(
                (list_len, time_len, block), lambda g, rows: (0, 0, 0)
            ),
        ),
        compiler_params=pltpu.CompilerParams(vmem_limit_bytes=32 * 1024 * 1024),
        name="products",
    )(rows, pressure, gathered)


def collect_kernel(count, dest_ref, in_ref, out_ref):
    out_ref[...] = jnp.zeros_like(out_ref)

    def step(e, carry):
        out_ref[dest_ref[e]] += in_ref[e].astype(jnp.float32)
        return carry

    lax.fori_loop(0, count, step, 0)


def collect(dest, received, capacity):
    count, time_len, block = received.shape
    return pl.pallas_call(
        functools.partial(collect_kernel, count),
        out_shape=jax.ShapeDtypeStruct((capacity, time_len, block), jnp.float32),
        grid_spec=pltpu.PrefetchScalarGridSpec(
            num_scalar_prefetch=1,
            grid=(1,),
            in_specs=[pl.BlockSpec(received.shape, lambda g, dest: (0, 0, 0))],
            out_specs=pl.BlockSpec(
                (capacity, time_len, block), lambda g, dest: (0, 0, 0)
            ),
        ),
        compiler_params=pltpu.CompilerParams(vmem_limit_bytes=32 * 1024 * 1024),
        name="collect",
    )(dest, received)


def tables(panel_list, owner_list, owner_count, own, slots):
    owners, list_len = panel_list.shape
    capacity = owner_list.shape[1]
    live = jnp.arange(capacity, dtype=jnp.int32)[None, :] < owner_count[:, None]
    listed = jnp.where(live, owner_list, -1).reshape(1, -1)
    place = jnp.arange(owners * capacity, dtype=jnp.int32)[None, :]
    found = jnp.sum(
        jnp.where(panel_list.reshape(-1, 1) == listed, place, 0), axis=1, dtype=jnp.int32
    ).reshape(owners, list_len)
    target, slot = found // capacity, found % capacity
    position = jnp.arange(list_len, dtype=jnp.int32)
    earlier = (target[:, None, :] == target[:, :, None]) & (
        position[None, None, :] < position[None, :, None]
    )
    rank = jnp.sum(earlier, axis=2, dtype=jnp.int32)
    packed_row = target * slots + rank
    wanted = own * slots + jnp.arange(slots, dtype=jnp.int32)
    dest = jnp.sum(
        jnp.where(packed_row[:, None, :] == wanted[None, :, None], slot[:, None, :], 0),
        axis=2,
        dtype=jnp.int32,
    )
    return packed_row[own], dest.reshape(-1)


def body(n_tm, n_owner, pressure, proj_weight, pattern, panel_list, owner_list, owner_count):
    own = lax.axis_index("owner")
    list_len = panel_list.shape[1]
    capacity = owner_list.shape[1]
    slots = list_len // n_owner
    packed_row, dest = tables(panel_list, owner_list, owner_count, own, slots)
    fb, kp = pattern.shape[1:]
    rows = packed_row[pattern[0].reshape(-1)].reshape(1, -1)
    rows = jnp.pad(rows, ((0, 7), (0, 128 - rows.shape[1])))
    gathered, rows = gather(proj_weight[0], rows, n_tm)
    rows = rows[:, 0, : fb * kp].reshape(-1)
    packed = products(rows, pressure, gathered, list_len)
    block_shape = packed.shape[1:]
    received = exchange(packed.reshape((n_owner, slots) + block_shape), n_owner)
    return collect(dest, received.reshape((list_len,) + block_shape), capacity)


def solution(mesh):
    placed = (
        P("tm", "owner"),
        P("owner", "tm", None, None, None),
        P("owner", "tm", None),
        P(),
        P(),
        P(),
    )
    return jax.shard_map(
        functools.partial(body, mesh.shape["tm"], mesh.shape["owner"]),
        mesh=mesh,
        in_specs=placed,
        out_specs=P("owner", "tm", None),
        check_vma=False,
    )
```

time: 398 us -> 117 us (0.29)
  waiting for transfers between devices: 264 us -> 0 us
  Pallas kernels: 0 us -> 106 us
  other arithmetic: 55.7 us -> 1.46 us
  local copies, waits for them, and re-layouts: 47 us -> 9.4 us
  between operations: 13.5 us -> 0.08 us
  starting transfers between devices: 11.9 us -> 0 us
  matrix products: 4.51 us -> 0 us
    reduce_scatter x1 -> x0, waiting for transfers between devices: 161 us -> none  [body(): return lax.psum_scatter(combined, 'tm', scatter_dimension=1, tiled=True)]
    pallas_call x0 -> x4, Pallas kernels: none -> 106 us  [the longest x1 73.1 us: gather(): pl.pallas_call(functools.partial(gather_kernel, n), out_shape=(jax.ShapeD...]
    all_to_all x2 -> x0, waiting for transfers between devices: 103 us -> none  [the longest x1 88 us: body(): lax.all_to_all(packed, 'owner', split_axis=0, concat_axis=0, tiled=True)]
    scatter-add x2 -> x0, other arithmetic: 37.7 us -> none  [the longest x1 18.9 us: collect(): combined = jax.ops.segment_sum(flat_rows, dest, num_segments=capacity + 1)]
    all_to_all x2 -> x0, starting transfers between devices: 11.9 us -> none  [the longest x1 6.45 us: body(): lax.all_to_all(packed, 'owner', split_axis=0, concat_axis=0, tiled=True)]
    broadcast_in_dim x2 -> x0, local copies, waits for them, and re-layouts: 9.08 us -> none  [the longest x1 4.86 us: collect(): combined = jax.ops.segment_sum(flat_rows, dest, num_segments=capacity + 1)]
    reshape x1, local copies, waits for them, and re-layouts: 8.95 us -> 0.08 us  [tables(): return (packed_row[own], dest.reshape(-1))]
    reduce_sum x4 -> x3, other arithmetic: 8.51 us -> 0.63 us  [the longest x1 0.29 us: tables(): rank = jnp.sum(earlier, axis=2, dtype=jnp.int32)]
  transfers between devices with their start and end apart: 3 -> 0, of which waited for: 3 -> 0; matrix products, arithmetic and copies ran while one was open for 3% -> 0% of each run, Pallas kernels for 0% -> 0%
where the time goes in v1:
time: 117 us
  Pallas kernels  106 us (91%)
  local copies, waits for them, and re-layouts  9.4 us (8%)
  other arithmetic  1.46 us (1%)
    pallas_call x1, Pallas kernels, gather(): pl.pallas_call(functools.partial(gather_kernel, n), out_shape=(jax.ShapeD...  73.1 us
    pallas_call x1, Pallas kernels, exchange(): pl.pallas_call(functools.partial(exchange_kernel, n), out_shape=jax.Shape...  27.9 us
    unnamed x9, local copies, waits for them, and re-layouts  5.85 us
    pallas_call x1, Pallas kernels, products(): pl.pallas_call(functools.partial(product_kernel, fb, kp), out_shape=jax.S...  2.62 us
    pallas_call x1, Pallas kernels, collect(): pl.pallas_call(functools.partial(collect_kernel, count), out_shape=jax.Sh...  2.43 us

profile of v1, /device:TPU:1, one launch (start us, length us, event | category | flops | bytes accessed | tf_op | source)
XLA Modules:
  0.0 116.9 jit_solution(18302580913059133936)
XLA Ops:
  0.0 0.0 copy-start.3
  0.0 0.9 eq.45
  0.9 0.8 copy.10
  1.6 0.1 reshape_squeeze.6
  1.7 0.8 fusion
  2.5 0.1 eq.47
  2.6 0.1 select_reduce_fusion
  2.7 0.1 ne.56
  2.8 0.1 div.21
  2.9 0.1 rem.33
  3.0 0.3 convert_reduce_fusion
  3.3 0.2 select_reduce_fusion.1
  3.5 0.7 gather_fusion
  4.2 0.1 copy.9
  4.3 0.1 reshape.126.dest_ref
  4.4 0.6 pad.4.pat_ref
  5.0 73.1 %gather_weights.1 = (bf16[4,8,4,128,128]{4,3,2,1,0:T(8,128)(2,1)}, s32[4,8,128]{2,1,0:T(8,128)}) custom-call(bf16[8,4,128,128]{3,2,1,0:T(8,128)(2,1)} %bitcast.10, s32[8,128]{1,0:T(8,128)} %pad.4.pat_ref), custom_call_target="tpu_custom_call" | custom-call | tf_op jit(solution)/shard_map/gather_weights/pallas_call | solution.py:119
  78.1 0.7 slice_reduce_fusion
  78.8 0.1 reshape_squeeze.7.rows_ref
  78.9 0.0 copy-done.3
  78.9 0.0 copy-start.2
  78.9 2.2 %copy-done.2 = bf16[4,8,4,128,128]{4,3,2,1,0:T(8,128)(2,1)S(1)} copy-done((bf16[4,8,4,128,128]{4,3,2,1,0:T(8,128)(2,1)S(1)}, bf16[4,8,4,128,128]{4,3,2,1,0:T(8,128)(2,1)}, u32[]{:S(2)}) %copy-start.2) | copy-done | bytes 4194328
  81.1 2.6 %products.1 = f32[32,128,128]{2,1,0:T(8,128)S(1)} custom-call(s32[128]{0:T(128)S(1)} %reshape_squeeze.7.rows_ref, bf16[128,4096]{1,0:T(8,128)(2,1)S(1)} %copy-done.3, bf16[4,8,4,128,128]{4,3,2,1,0:T(8,128)(2,1)S(1)} %copy-done.2), custom_call_target="tpu_custom_call" | custom-call | tf_op jit(solution)/shard_map/products/pallas_call | solution.py:204
  83.7 0.0 copy-start.1
  83.7 1.3 %copy-done.1 = f32[32,128,128]{2,1,0:T(8,128)} copy-done((f32[32,128,128]{2,1,0:T(8,128)}, f32[32,128,128]{2,1,0:T(8,128)S(1)}, u32[]{:S(2)}) %copy-start.1) | copy-done | bytes 2097176
  85.1 27.9 %exchange_sums.1 = f32[8,4,128,128]{3,2,1,0:T(8,128)} custom-call(f32[8,4,128,128]{3,2,1,0:T(8,128)} %bitcast.9), custom_call_target="tpu_custom_call" | custom-call | tf_op jit(solution)/shard_map/exchange_sums/pallas_call | solution.py:171
  112.9 0.0 copy-start
  112.9 1.6 %copy-done = f32[8,4,128,128]{3,2,1,0:T(8,128)S(1)} copy-done((f32[8,4,128,128]{3,2,1,0:T(8,128)S(1)}, f32[8,4,128,128]{3,2,1,0:T(8,128)}, u32[]{:S(2)}) %copy-start) | copy-done | bytes 2097176
  114.5 2.4 %collect.1 = f32[36,128,128]{2,1,0:T(8,128)} custom-call(s32[32]{0:T(128)S(1)} %reshape.126.dest_ref, f32[32,128,128]{2,1,0:T(8,128)S(1)} %bitcast.8), custom_call_target="tpu_custom_call" | custom-call | tf_op jit(solution)/shard_map/collect/pallas_call | solution.py:235
  (9 shorter events, 0.1 us)
Async XLA Ops:
  0.0 78.9 %copy-start.3 = (bf16[128,4096]{1,0:T(8,128)(2,1)S(1)}, bf16[128,4096]{1,0:T(8,128)(2,1)}, u32[]{:S(2)}) copy-start(bf16[128,4096]{1,0:T(8,128)(2,1)} %p_ref.1) | copy-start | bytes 3145732
  78.9 2.2 %copy-start.2 = (bf16[4,8,4,128,128]{4,3,2,1,0:T(8,128)(2,1)S(1)}, bf16[4,8,4,128,128]{4,3,2,1,0:T(8,128)(2,1)}, u32[]{:S(2)}) copy-start(bf16[4,8,4,128,128]{4,3,2,1,0:T(8,128)(2,1)} %get-tuple-element.8.w_ref) | copy-start | bytes 12582916
  83.7 1.3 %copy-start.1 = (f32[32,128,128]{2,1,0:T(8,128)}, f32[32,128,128]{2,1,0:T(8,128)S(1)}, u32[]{:S(2)}) copy-start(f32[32,128,128]{2,1,0:T(8,128)S(1)} %products.1) | copy-start | bytes 6291460
  112.9 1.6 %copy-start = (f32[8,4,128,128]{3,2,1,0:T(8,128)S(1)}, f32[8,4,128,128]{3,2,1,0:T(8,128)}, u32[]{:S(2)}) copy-start(f32[8,4,128,128]{3,2,1,0:T(8,128)} %exchange_sums.1) | copy-start | bytes 6291460

commit v2 on v0

v2 whole, which is shorter than its diff:
```python
import functools

import jax
import jax.numpy as jnp
from jax import lax
from jax.experimental import pallas as pl
from jax.experimental.pallas import tpu as pltpu
from jax.sharding import PartitionSpec as P

MESH = pl.DeviceIdType.MESH
PIECES = 4


def turn_kernel(n, w_ref, pat_ref, wt_ref, pg_ref, send_sem, recv_sem):
    m = lax.axis_index("tm")
    barrier = pltpu.get_barrier_semaphore()
    for step in range(1, n):
        pl.semaphore_signal(
            barrier, inc=1, device_id={"tm": lax.rem(m + step, n)}, device_id_type=MESH
        )
    pl.semaphore_wait(barrier, n - 1)

    def copy(step, landing):
        return pltpu.make_async_remote_copy(
            src_ref=pat_ref,
            dst_ref=pg_ref.at[landing],
            send_sem=send_sem.at[step],
            recv_sem=recv_sem.at[step],
            device_id={"tm": lax.rem(m + step, n)},
            device_id_type=MESH,
        )

    for step in range(1, n):
        copy(step, m).start()
    pg_ref[m] = pat_ref[...]
    rows = w_ref.shape[-1] // PIECES
    kp = w_ref.shape[1]

    def turn(i, carry):
        for k in range(kp):
            t = w_ref[i, k].T
            for c in range(PIECES):
                wt_ref[c, i, k] = t[c * rows : (c + 1) * rows]
        return carry

    lax.fori_loop(0, w_ref.shape[0], turn, 0)
    for step in range(1, n):
        copy(step, lax.rem(m - step + n, n)).wait_recv()
        copy(step, m).wait_send()


def turn(weights, pattern, n):
    fb, kp, faces, panels = weights.shape
    vmem = pl.BlockSpec(memory_space=pltpu.VMEM)
    return pl.pallas_call(
        functools.partial(turn_kernel, n),
        out_shape=(
            jax.ShapeDtypeStruct((PIECES, fb, kp, panels // PIECES, faces), weights.dtype),
            jax.ShapeDtypeStruct((n,) + pattern.shape, pattern.dtype),
        ),
        in_specs=[vmem] * 2,
        out_specs=(vmem, vmem),
        scratch_shapes=[
            pltpu.SemaphoreType.DMA((n,)),
            pltpu.SemaphoreType.DMA((n,)),
        ],
        compiler_params=pltpu.CompilerParams(
            collective_id=0, has_side_effects=True, vmem_limit_bytes=32 * 1024 * 1024
        ),
        name="turn_weights",
    )(weights, pattern)


def fused_kernel(
    n, owners, hit_ref, last_ref, w_ref, p_ref, out_ref,
    wg, terms, runs, outgoing, wsend, wrecv, osend, orecv, own_sem,
):
    m = lax.axis_index("tm")
    me = lax.axis_index("owner")
    pieces, fb, kp, rows, block = w_ref.shape
    time_len = p_ref.shape[0]
    hits = terms.shape[0]
    slots = out_ref.shape[1]

    barrier = pltpu.get_barrier_semaphore()
    for step in range(1, n):
        pl.semaphore_signal(
            barrier, inc=1, device_id={"tm": lax.rem(m + step, n)}, device_id_type=MESH
        )
    for step in range(1, owners):
        pl.semaphore_signal(
            barrier, inc=1, device_id={"owner": lax.rem(me + step, owners)}, device_id_type=MESH
        )
    pl.semaphore_wait(barrier, n + owners - 2)

    def origin_of(way, hop):
        return jnp.clip(m - hop if way == 0 else m + hop, 0, n - 1)

    def send(way, hop, c):
        origin = origin_of(way, hop)
        toward = m + 1 if way == 0 else m - 1
        return pltpu.make_async_remote_copy(
            src_ref=w_ref.at[c] if hop == 0 else wg.at[c, origin],
            dst_ref=wg.at[c, origin],
            send_sem=wsend.at[way, hop, c],
            recv_sem=wrecv.at[way, hop, c],
            device_id={"tm": jnp.clip(toward, 0, n - 1)},
            device_id_type=MESH,
        )

    def landed(way, hop, c):
        return pltpu.make_async_remote_copy(
            src_ref=w_ref.at[c],
            dst_ref=wg.at[c, origin_of(way, hop + 1)],
            send_sem=wsend.at[way, hop, c],
            recv_sem=wrecv.at[way, hop, c],
            device_id={"tm": lax.rem(m + 1, n)},
            device_id_type=MESH,
        )

    def sends(way, hop):
        return (m - hop >= 0) & (m + 1 < n) if way == 0 else (m + hop < n) & (m >= 1)

    def lands(way, hop):
        return m - 1 - hop >= 0 if way == 0 else m + 1 + hop < n

    def start_own(c):
        for way in range(2):
            @pl.when(sends(way, 0))
            def _():
                send(way, 0, c).start()

    def product(weights, origin):
        for i in range(fb):
            face = origin * fb + i
            x = p_ref[:, pl.ds(pl.multiple_of(face * block, block), block)]
            y = lax.dot_general(
                weights(i).reshape(kp * rows, block), x, (((1,), (1,)), ((), ())),
                preferred_element_type=jnp.float32,
            )
            terms[pl.ds(face * kp, kp)] = y.reshape(kp, rows, time_len)

    def give(c, step, landing):
        peer = lax.rem(me + step, owners)
        return pltpu.make_async_remote_copy(
            src_ref=outgoing.at[c, peer],
            dst_ref=out_ref.at[landing, :, c],
            send_sem=osend.at[c, step],
            recv_sem=orecv.at[c, step],
            device_id={"owner": peer},
            device_id_type=MESH,
        )

    def keep(c):
        return pltpu.make_async_copy(outgoing.at[c, me], out_ref.at[me, :, c], own_sem.at[c])

    for c in range(min(2, pieces)):
        start_own(c)

    def piece(c, carry):
        product(lambda i: w_ref[c, i], m)
        for hop in range(n - 1):
            for way in range(2):
                @pl.when(lands(way, hop))
                def _():
                    landed(way, hop, c).wait_recv()
                if hop + 1 < n - 1:
                    @pl.when(sends(way, hop + 1))
                    def _():
                        send(way, hop + 1, c).start()
            if hop == 0:
                @pl.when(c + 2 < pieces)
                def _():
                    start_own(c + 2)
            for way in range(2):
                @pl.when(lands(way, hop))
                def _():
                    origin = origin_of(way, hop + 1)
                    product(lambda i: wg[c, origin, i], origin)

        def run(h, total):
            code = hit_ref[h]
            term = terms[code >> 1]
            total = jnp.where((code & 1) == 1, term, total + term)
            runs[h] = total
            return total

        lax.fori_loop(0, hits, run, jnp.zeros((rows, time_len), jnp.float32), unroll=8)
        for peer in range(owners):
            for slot in range(slots):
                code = last_ref[peer * slots + slot]
                total = runs[code >> 1]
                outgoing[c, peer, slot] = jnp.where((code & 1) == 1, total, jnp.zeros_like(total))
        for step in range(1, owners):
            give(c, step, me).start()
        keep(c).start()
        return carry

    lax.fori_loop(0, pieces, piece, 0)

    def finish(c, carry):
        for hop in range(n - 1):
            for way in range(2):
                @pl.when(sends(way, hop))
                def _():
                    send(way, hop, c).wait_send()
        for step in range(1, owners):
            give(c, step, lax.rem(me - step + owners, owners)).wait_recv()
            give(c, step, me).wait_send()
        keep(c).wait()
        return carry

    lax.fori_loop(0, pieces, finish, 0)


def fused(hit, last, turned, pressure, n, owners):
    pieces, fb, kp, rows, block = turned.shape
    time_len = pressure.shape[0]
    slots = last.shape[0] // owners
    hits = hit.shape[0]
    smem = pl.BlockSpec(memory_space=pltpu.SMEM)
    vmem = pl.BlockSpec(memory_space=pltpu.VMEM)
    return pl.pallas_call(
        functools.partial(fused_kernel, n, owners),
        out_shape=jax.ShapeDtypeStruct((owners, slots, pieces, rows, time_len), jnp.float32),
        in_specs=[smem, smem, vmem, vmem],
        out_specs=pl.BlockSpec(memory_space=pl.ANY),
        scratch_shapes=[
            pltpu.VMEM((pieces, n, fb, kp, rows, block), turned.dtype),
            pltpu.VMEM((hits, rows, time_len), jnp.float32),
            pltpu.VMEM((hits, rows, time_len), jnp.float32),
            pltpu.VMEM((pieces, owners, slots, rows, time_len), jnp.float32),
            pltpu.SemaphoreType.DMA((2, n - 1, pieces)),
            pltpu.SemaphoreType.DMA((2, n - 1, pieces)),
            pltpu.SemaphoreType.DMA((pieces, owners)),
            pltpu.SemaphoreType.DMA((pieces, owners)),
            pltpu.SemaphoreType.DMA((pieces,)),
        ],
        compiler_params=pltpu.CompilerParams(
            collective_id=1, has_side_effects=True, vmem_limit_bytes=48 * 1024 * 1024
        ),
        name="gather_multiply_exchange",
    )(hit, last, turned, pressure)


def hit_tables(rows, count):
    order = jnp.arange(rows.shape[0], dtype=jnp.int32)
    same = rows[:, None] == rows[None, :]
    before = order[None, :] < order[:, None]
    ahead = (rows[None, :] < rows[:, None]) | (same & before)
    rank = jnp.sum(ahead, axis=1, dtype=jnp.int32)
    first = 1 - jnp.any(same & before, axis=1).astype(jnp.int32)
    code = 2 * order + first
    hit = jnp.sum(
        jnp.where(rank[:, None] == order[None, :], code[:, None], 0), axis=0, dtype=jnp.int32
    )
    wanted = jnp.arange(count, dtype=jnp.int32)
    upto = jnp.sum(rows[None, :] <= wanted[:, None], axis=1, dtype=jnp.int32)
    there = jnp.any(rows[None, :] == wanted[:, None], axis=1).astype(jnp.int32)
    return hit, 2 * jnp.maximum(upto - 1, 0) + there


def collect_kernel(count, dest_ref, in_ref, out_ref):
    out_ref[...] = jnp.zeros_like(out_ref)

    def step(e, carry):
        out_ref[dest_ref[e]] += in_ref[e].T
        return carry

    lax.fori_loop(0, count, step, 0)


def collect(dest, received, capacity):
    count, block, time_len = received.shape
    return pl.pallas_call(
        functools.partial(collect_kernel, count),
        out_shape=jax.ShapeDtypeStruct((capacity, time_len, block), jnp.float32),
        grid_spec=pltpu.PrefetchScalarGridSpec(
            num_scalar_prefetch=1,
            grid=(1,),
            in_specs=[pl.BlockSpec(received.shape, lambda g, dest: (0, 0, 0))],
            out_specs=pl.BlockSpec(
                (capacity, time_len, block), lambda g, dest: (0, 0, 0)
            ),
        ),
        compiler_params=pltpu.CompilerParams(vmem_limit_bytes=32 * 1024 * 1024),
        name="collect",
    )(dest, received)


def tables(panel_list, owner_list, owner_count, own, slots):
    owners, list_len = panel_list.shape
    capacity = owner_list.shape[1]
    live = jnp.arange(capacity, dtype=jnp.int32)[None, :] < owner_count[:, None]
    listed = jnp.where(live, owner_list, -1).reshape(1, -1)
    place = jnp.arange(owners * capacity, dtype=jnp.int32)[None, :]
    found = jnp.sum(
        jnp.where(panel_list.reshape(-1, 1) == listed, place, 0), axis=1, dtype=jnp.int32
    ).reshape(owners, list_len)
    target, slot = found // capacity, found % capacity
    position = jnp.arange(list_len, dtype=jnp.int32)
    earlier = (target[:, None, :] == target[:, :, None]) & (
        position[None, None, :] < position[None, :, None]
    )
    rank = jnp.sum(earlier, axis=2, dtype=jnp.int32)
    packed_row = target * slots + rank
    wanted = own * slots + jnp.arange(slots, dtype=jnp.int32)
    dest = jnp.sum(
        jnp.where(packed_row[:, None, :] == wanted[None, :, None], slot[:, None, :], 0),
        axis=2,
        dtype=jnp.int32,
    )
    return packed_row[own], dest.reshape(-1)


def body(n_tm, n_owner, pressure, proj_weight, pattern, panel_list, owner_list, owner_count):
    own = lax.axis_index("owner")
    list_len = panel_list.shape[1]
    capacity = owner_list.shape[1]
    slots = list_len // n_owner
    packed_row, dest = tables(panel_list, owner_list, owner_count, own, slots)
    fb, kp = pattern.shape[1:]
    rows = packed_row[pattern[0].reshape(-1)].reshape(1, -1)
    rows = jnp.pad(rows, ((0, 7), (0, 128 - rows.shape[1])))
    turned, rows = turn(proj_weight[0], rows, n_tm)
    rows = rows[:, 0, : fb * kp].reshape(-1)
    hit, last = hit_tables(rows, list_len)
    received = fused(hit, last, turned, pressure, n_tm, n_owner)
    time_len = pressure.shape[0]
    return collect(dest, received.reshape(list_len, -1, time_len), capacity)


def solution(mesh):
    placed = (
        P("tm", "owner"),
        P("owner", "tm", None, None, None),
        P("owner", "tm", None),
        P(),
        P(),
        P(),
    )
    return jax.shard_map(
        functools.partial(body, mesh.shape["tm"], mesh.shape["owner"]),
        mesh=mesh,
        in_specs=placed,
        out_specs=P("owner", "tm", None),
        check_vma=False,
    )
```

time: 398 us -> 99.7 us (0.25)
  waiting for transfers between devices: 264 us -> 0 us
  Pallas kernels: 0 us -> 92.3 us
  other arithmetic: 55.7 us -> 2.17 us
  local copies, waits for them, and re-layouts: 47 us -> 4.21 us
  between operations: 13.5 us -> 0.11 us
  starting transfers between devices: 11.9 us -> 0 us
  matrix products: 4.51 us -> 0 us
    reduce_scatter x1 -> x0, waiting for transfers between devices: 161 us -> none  [body(): return lax.psum_scatter(combined, 'tm', scatter_dimension=1, tiled=True)]
    all_to_all x2 -> x0, waiting for transfers between devices: 103 us -> none  [the longest x1 88 us: body(): lax.all_to_all(packed, 'owner', split_axis=0, concat_axis=0, tiled=True)]
    pallas_call x0 -> x3, Pallas kernels: none -> 92.3 us  [the longest x1 81.4 us: fused(): pl.pallas_call(functools.partial(fused_kernel, n, owners), out_shape=jax....]
    scatter-add x2 -> x0, other arithmetic: 37.7 us -> none  [the longest x1 18.9 us: collect(): combined = jax.ops.segment_sum(flat_rows, dest, num_segments=capacity + 1)]
    all_to_all x2 -> x0, starting transfers between devices: 11.9 us -> none  [the longest x1 6.45 us: body(): lax.all_to_all(packed, 'owner', split_axis=0, concat_axis=0, tiled=True)]
    broadcast_in_dim x2 -> x0, local copies, waits for them, and re-layouts: 9.08 us -> none  [the longest x1 4.86 us: collect(): combined = jax.ops.segment_sum(flat_rows, dest, num_segments=capacity + 1)]
    reshape x1, local copies, waits for them, and re-layouts: 8.95 us -> 0.08 us  [tables(): return (packed_row[own], dest.reshape(-1))]
    slice x1, local copies, waits for them, and re-layouts: 8.43 us -> 0.02 us  [body(): rows = rows[:, 0, :fb * kp].reshape(-1)]
  transfers between devices with their start and end apart: 3 -> 0, of which waited for: 3 -> 0; matrix products, arithmetic and copies ran while one was open for 3% -> 0% of each run, Pallas kernels for 0% -> 0%
where the time goes in v2:
time: 99.7 us; the launch traced here: 98.8 us
  Pallas kernels  92.3 us (93%)
  local copies, waits for them, and re-layouts  4.21 us (4%)
  other arithmetic  2.17 us (2%)
    pallas_call x1, Pallas kernels, fused(): pl.pallas_call(functools.partial(fused_kernel, n, owners), out_shape=jax....  81.4 us
    pallas_call x1, Pallas kernels, turn(): pl.pallas_call(functools.partial(turn_kernel, n), out_shape=(jax.ShapeDty...  5.54 us
    pallas_call x1, Pallas kernels, collect(): pl.pallas_call(functools.partial(collect_kernel, count), out_shape=jax.Sh...  5.33 us

profile of v2, /device:TPU:1, one launch (start us, length us, event | category | flops | bytes accessed | tf_op | source)
XLA Modules:
  0.0 98.8 jit_solution(5108082545999756932)
XLA Ops:
  0.0 0.0 copy-start
  0.0 0.9 eq.32
  0.9 0.8 copy.10
  1.6 0.1 reshape_squeeze.3
  1.7 0.8 fusion.3
  2.5 0.1 eq.34
  2.6 0.1 select_reduce_fusion
  2.7 0.1 ne.56
  2.8 0.1 div.21
  2.9 0.1 rem.33
  3.0 0.3 convert_reduce_fusion
  3.3 0.2 select_reduce_fusion.2
  3.5 0.7 gather_fusion
  4.2 0.1 copy.9
  4.3 0.1 reshape.135.dest_ref
  4.4 0.0 copy-start.1
  4.4 1.2 %copy-done.1 = bf16[1,8,4,128,128]{4,3,2,1,0:T(8,128)(2,1)S(1)} copy-done((bf16[1,8,4,128,128]{4,3,2,1,0:T(8,128)(2,1)S(1)}, bf16[1,8,4,128,128]{4,3,2,1,0:T(8,128)(2,1)}, u32[]{:S(2)}) %copy-start.1) | copy-done | bytes 1048600
  5.6 5.5 %turn_weights.1 = (bf16[4,8,4,32,128]{4,3,2,1,0:T(8,128)(2,1)S(1)}, s32[4,8,128]{2,1,0:T(8,128)S(1)}) custom-call(bf16[8,4,128,128]{3,2,1,0:T(8,128)(2,1)S(1)} %bitcast.8, s32[8,128]{1,0:T(8,128)S(1)} %pad.4.pat_ref), custom_call_target="tpu_custom_call" | custom-call | tf_op jit(solution)/shard_map/turn_weights/pallas_call | solution.py:55
  11.2 0.1 lt.89
  11.3 0.1 fusion.2
  11.4 0.1 convert_reduce_fusion.2
  11.5 0.2 fusion.1
  11.7 0.2 convert_reduce_fusion.1
  11.9 0.1 select_reduce_fusion.1.hit_ref
  12.0 0.0 copy-done
  12.0 81.4 %gather_multiply_exchange.1 = f32[8,4,4,32,128]{4,3,2,1,0:T(8,128)S(1)} custom-call(s32[128]{0:T(128)S(1)} %select_reduce_fusion.1.hit_ref, s32[32]{0:T(128)S(1)} %convert_add_fusion.last_ref, bf16[4,8,4,32,128]{4,3,2,1,0:T(8,128)(2,1)S(1)} %get-tuple-element.8.w_ref, bf16[128,4096]{1,0:T(8,128)(2,1)S(1)} %copy-done), custom_call_target="tpu_custom_call" | custom-call | tf_op jit(solution)/shard_map/gather_multiply_exchange/pallas_call | solution.py:223
  93.5 5.3 %collect.1 = f32[36,128,128]{2,1,0:T(8,128)} custom-call(s32[32]{0:T(128)S(1)} %reshape.135.dest_ref, f32[32,128,128]{2,1,0:T(8,128)S(1)} %bitcast.7), custom_call_target="tpu_custom_call" | custom-call | tf_op jit(solution)/shard_map/collect/pallas_call | solution.py:275
  (13 shorter events, 0.1 us)
Async XLA Ops:
  0.0 12.0 %copy-start = (bf16[128,4096]{1,0:T(8,128)(2,1)S(1)}, bf16[128,4096]{1,0:T(8,128)(2,1)}, u32[]{:S(2)}) copy-start(bf16[128,4096]{1,0:T(8,128)(2,1)} %p_ref.1) | copy-start | bytes 3145732
  4.4 1.2 %copy-start.1 = (bf16[1,8,4,128,128]{4,3,2,1,0:T(8,128)(2,1)S(1)}, bf16[1,8,4,128,128]{4,3,2,1,0:T(8,128)(2,1)}, u32[]{:S(2)}) copy-start(bf16[1,8,4,128,128]{4,3,2,1,0:T(8,128)(2,1)} %param.7) | copy-start | bytes 3145732

commit v3 on v2

--- a/solution.py
+++ b/solution.py
@@ -9,6 +9,7 @@
 
 MESH = pl.DeviceIdType.MESH
 PIECES = 4
+LOCAL = 2
 
 
 def turn_kernel(n, w_ref, pat_ref, wt_ref, pg_ref, send_sem, recv_sem):
@@ -73,7 +74,7 @@
 
 def fused_kernel(
     n, owners, hit_ref, last_ref, w_ref, p_ref, out_ref,
-    wg, terms, runs, outgoing, wsend, wrecv, osend, orecv, own_sem,
+    wg, terms, runs, outgoing, lent, outgoing2, wsend, wrecv, osend, orecv, own_sem, lent_sem, osend2,
 ):
     m = lax.axis_index("tm")
     me = lax.axis_index("owner")
@@ -91,7 +92,30 @@
         pl.semaphore_signal(
             barrier, inc=1, device_id={"owner": lax.rem(me + step, owners)}, device_id_type=MESH
         )
-    pl.semaphore_wait(barrier, n + owners - 2)
+    is_end = (m == 0) | (m == n - 1)
+    helps = (m == 1) | (m == n - 2)
+    near = jnp.where(m < n // 2, 1, n - 2)
+    far = jnp.where(m < n // 2, 0, n - 1)
+
+    @pl.when(is_end)
+    def _():
+        for step in range(owners):
+            pl.semaphore_signal(
+                barrier, inc=1, device_id={"tm": near, "owner": lax.rem(me + step, owners)},
+                device_id_type=MESH,
+            )
+
+    pl.semaphore_wait(barrier, n + owners - 2 + jnp.where(helps, owners, 0))
+
+    def lend():
+        return pltpu.make_async_remote_copy(
+            src_ref=p_ref,
+            dst_ref=lent,
+            send_sem=lent_sem.at[0],
+            recv_sem=lent_sem.at[1],
+            device_id={"tm": near},
+            device_id_type=MESH,
+        )
 
     def origin_of(way, hop):
         return jnp.clip(m - hop if way == 0 else m + hop, 0, n - 1)
@@ -118,19 +142,26 @@
             device_id_type=MESH,
         )
 
-    def sends(way, hop):
-        return (m - hop >= 0) & (m + 1 < n) if way == 0 else (m + hop < n) & (m >= 1)
-
-    def lands(way, hop):
-        return m - 1 - hop >= 0 if way == 0 else m + 1 + hop < n
+    def edge(c):
+        return jnp.where(c >= LOCAL, 1, 0)
+
+    def sends(way, hop, c):
+        if way == 0:
+            return (m - hop >= 0) & (m + 1 < n - edge(c))
+        return (m + hop < n) & (m - 1 >= edge(c))
+
+    def lands(way, hop, c):
+        if way == 0:
+            return (m - 1 - hop >= 0) & (m < n - edge(c))
+        return (m + 1 + hop < n) & (m >= edge(c))
 
     def start_own(c):
         for way in range(2):
-            @pl.when(sends(way, 0))
+            @pl.when(sends(way, 0, c))
             def _():
                 send(way, 0, c).start()
 
-    def product(weights, origin):
+    def product(weights, origin, p_ref):
         for i in range(fb):
             face = origin * fb + i
             x = p_ref[:, pl.ds(pl.multiple_of(face * block, block), block)]
@@ -154,63 +185,126 @@
     def keep(c):
         return pltpu.make_async_copy(outgoing.at[c, me], out_ref.at[me, :, c], own_sem.at[c])
 
-    for c in range(min(2, pieces)):
-        start_own(c)
-
-    def piece(c, carry):
-        product(lambda i: w_ref[c, i], m)
-        for hop in range(n - 1):
-            for way in range(2):
-                @pl.when(lands(way, hop))
-                def _():
-                    landed(way, hop, c).wait_recv()
-                if hop + 1 < n - 1:
-                    @pl.when(sends(way, hop + 1))
-                    def _():
-                        send(way, hop + 1, c).start()
-            if hop == 0:
-                @pl.when(c + 2 < pieces)
-                def _():
-                    start_own(c + 2)
-            for way in range(2):
-                @pl.when(lands(way, hop))
-                def _():
-                    origin = origin_of(way, hop + 1)
-                    product(lambda i: wg[c, origin, i], origin)
-
-        def run(h, total):
-            code = hit_ref[h]
-            term = terms[code >> 1]
-            total = jnp.where((code & 1) == 1, term, total + term)
-            runs[h] = total
-            return total
-
+    def give2(c, step, landing):
+        peer = lax.rem(me + step, owners)
+        return pltpu.make_async_remote_copy(
+            src_ref=outgoing2.at[jnp.maximum(c - LOCAL, 0), peer],
+            dst_ref=out_ref.at[landing, :, c],
+            send_sem=osend2.at[c, step],
+            recv_sem=orecv.at[c, step],
+            device_id={"tm": far, "owner": peer},
+            device_id_type=MESH,
+        )
+
+    def run(h, total):
+        code = hit_ref[h]
+        term = terms[code >> 1]
+        total = jnp.where((code & 1) == 1, term, total + term)
+        runs[h] = total
+        return total
+
+    def sum_up(target, at):
         lax.fori_loop(0, hits, run, jnp.zeros((rows, time_len), jnp.float32), unroll=8)
         for peer in range(owners):
             for slot in range(slots):
                 code = last_ref[peer * slots + slot]
                 total = runs[code >> 1]
-                outgoing[c, peer, slot] = jnp.where((code & 1) == 1, total, jnp.zeros_like(total))
-        for step in range(1, owners):
-            give(c, step, me).start()
-        keep(c).start()
-        return carry
-
-    lax.fori_loop(0, pieces, piece, 0)
-
-    def finish(c, carry):
+                target[at, peer, slot] = jnp.where((code & 1) == 1, total, jnp.zeros_like(total))
+
+    for c in range(LOCAL):
+        start_own(c)
+
+    @pl.when(is_end)
+    def _():
+        lend().start()
+
+    def piece(c, carry):
+        at_home = jnp.logical_not(is_end) | (c < LOCAL)
+
+        @pl.when(at_home)
+        def _():
+            product(lambda i: w_ref[c, i], m, p_ref)
+
         for hop in range(n - 1):
             for way in range(2):
-                @pl.when(sends(way, hop))
+                @pl.when(lands(way, hop, c))
+                def _():
+                    landed(way, hop, c).wait_recv()
+                if hop + 1 < n - 1:
+                    @pl.when(sends(way, hop + 1, c))
+                    def _():
+                        send(way, hop + 1, c).start()
+            if hop == 0:
+                @pl.when(c + LOCAL < pieces)
+                def _():
+                    start_own(c + LOCAL)
+            for way in range(2):
+                @pl.when(lands(way, hop, c))
+                def _():
+                    origin = origin_of(way, hop + 1)
+                    product(lambda i: wg[c, origin, i], origin, p_ref)
+
+        @pl.when(at_home)
+        def _():
+            sum_up(outgoing, c)
+            for step in range(1, owners):
+                give(c, step, me).start()
+            keep(c).start()
+
+        @pl.when(helps & (c == LOCAL))
+        def _():
+            lend().wait_recv()
+
+        @pl.when(helps & (c >= LOCAL))
+        def _():
+            product(lambda i: w_ref[c, i], m, lent)
+
+            def other(step, carry):
+                origin = lax.rem(m + step, n)
+                product(lambda i: wg[c, origin, i], origin, lent)
+                return carry
+
+            lax.fori_loop(1, n, other, 0)
+            sum_up(outgoing2, c - LOCAL)
+            for step in range(owners):
+                give2(c, step, me).start()
+
+        return carry
+
+    lax.fori_loop(0, pieces, piece, 0)
+
+    def finish(c, carry):
+        at_home = jnp.logical_not(is_end) | (c < LOCAL)
+        for hop in range(n - 1):
+            for way in range(2):
+                @pl.when(sends(way, hop, c))
                 def _():
                     send(way, hop, c).wait_send()
         for step in range(1, owners):
             give(c, step, lax.rem(me - step + owners, owners)).wait_recv()
-            give(c, step, me).wait_send()
-        keep(c).wait()
+
+        @pl.when(at_home)
+        def _():
+            for step in range(1, owners):
+                give(c, step, me).wait_send()
+            keep(c).wait()
+
+        @pl.when(jnp.logical_not(at_home))
+        def _():
+            give2(c, 0, me).wait_recv()
+
+        @pl.when(helps & (c >= LOCAL))
+        def _():
+            for step in range(owners):
+                give2(c, step, me).wait_send()
+
         return carry
 
     lax.fori_loop(0, pieces, finish, 0)
+
+    @pl.when(is_end)
+    def _():
+        lend().wait_send()
 
 
 def fused(hit, last, turned, pressure, n, owners):
@@ -230,11 +324,15 @@
             pltpu.VMEM((hits, rows, time_len), jnp.float32),
             pltpu.VMEM((hits, rows, time_len), jnp.float32),
             pltpu.VMEM((pieces, owners, slots, rows, time_len), jnp.float32),
+            pltpu.VMEM(pressure.shape, pressure.dtype),
+            pltpu.VMEM((pieces - LOCAL, owners, slots, rows, time_len), jnp.float32),
             pltpu.SemaphoreType.DMA((2, n - 1, pieces)),
             pltpu.SemaphoreType.DMA((2, n - 1, pieces)),
             pltpu.SemaphoreType.DMA((pieces, owners)),
             pltpu.SemaphoreType.DMA((pieces, owners)),
             pltpu.SemaphoreType.DMA((pieces,)),
+            pltpu.SemaphoreType.DMA((2,)),
+            pltpu.SemaphoreType.DMA((pieces, owners)),
         ],
         compiler_params=pltpu.CompilerParams(
             collective_id=1, has_side_effects=True, vmem_limit_bytes=48 * 1024 * 1024

time: 99.7 us -> 98.3 us (0.986)
  no operation moved by 1% of the time
where the time goes in v3:
time: 98.3 us; the launch traced here: 98 us
  Pallas kernels  91.5 us (93%)
  local copies, waits for them, and re-layouts  4.21 us (4%)
  other arithmetic  2.17 us (2%)
    pallas_call x1, Pallas kernels, fused(): pl.pallas_call(functools.partial(fused_kernel, n, owners), out_shape=jax....  80.7 us
    pallas_call x1, Pallas kernels, turn(): pl.pallas_call(functools.partial(turn_kernel, n), out_shape=(jax.ShapeDty...  5.54 us
    pallas_call x1, Pallas kernels, collect(): pl.pallas_call(functools.partial(collect_kernel, count), out_shape=jax.Sh...  5.33 us
    unnamed x5, local copies, waits for them, and re-layouts  1.98 us

profile of v3, /device:TPU:1, one launch (start us, length us, event | category | flops | bytes accessed | tf_op | source)
XLA Modules:
  0.0 98.0 jit_solution(794179233128630538)
XLA Ops:
  0.0 0.0 copy-start
  0.0 0.9 eq.32
  0.9 0.8 copy.10
  1.6 0.1 reshape_squeeze.3
  1.7 0.8 fusion.3
  2.5 0.1 eq.34
  2.6 0.1 select_reduce_fusion
  2.7 0.1 ne.56
  2.8 0.1 div.21
  2.9 0.1 rem.33
  3.0 0.3 convert_reduce_fusion
  3.3 0.2 select_reduce_fusion.2
  3.5 0.7 gather_fusion
  4.2 0.1 copy.9
  4.3 0.1 reshape.135.dest_ref
  4.4 0.0 copy-start.1
  4.4 1.2 %copy-done.1 = bf16[1,8,4,128,128]{4,3,2,1,0:T(8,128)(2,1)S(1)} copy-done((bf16[1,8,4,128,128]{4,3,2,1,0:T(8,128)(2,1)S(1)}, bf16[1,8,4,128,128]{4,3,2,1,0:T(8,128)(2,1)}, u32[]{:S(2)}) %copy-start.1) | copy-done | bytes 1048600
  5.6 5.5 %turn_weights.1 = (bf16[4,8,4,32,128]{4,3,2,1,0:T(8,128)(2,1)S(1)}, s32[4,8,128]{2,1,0:T(8,128)S(1)}) custom-call(bf16[8,4,128,128]{3,2,1,0:T(8,128)(2,1)S(1)} %bitcast.8, s32[8,128]{1,0:T(8,128)S(1)} %pad.4.pat_ref), custom_call_target="tpu_custom_call" | custom-call | tf_op jit(solution)/shard_map/turn_weights/pallas_call | solution.py:56
  11.2 0.1 lt.89
  11.3 0.1 fusion.2
  11.4 0.1 convert_reduce_fusion.2
  11.5 0.2 fusion.1
  11.7 0.2 convert_reduce_fusion.1
  11.9 0.1 select_reduce_fusion.1.hit_ref
  12.0 0.0 copy-done
  12.0 80.7 %gather_multiply_exchange.1 = f32[8,4,4,32,128]{4,3,2,1,0:T(8,128)S(1)} custom-call(s32[128]{0:T(128)S(1)} %select_reduce_fusion.1.hit_ref, s32[32]{0:T(128)S(1)} %convert_add_fusion.last_ref, bf16[4,8,4,32,128]{4,3,2,1,0:T(8,128)(2,1)S(1)} %get-tuple-element.8.w_ref, bf16[128,4096]{1,0:T(8,128)(2,1)S(1)} %copy-done), custom_call_target="tpu_custom_call" | custom-call | tf_op jit(solution)/shard_map/gather_multiply_exchange/pallas_call | solution.py:317
  92.7 5.3 %collect.1 = f32[36,128,128]{2,1,0:T(8,128)} custom-call(s32[32]{0:T(128)S(1)} %reshape.135.dest_ref, f32[32,128,128]{2,1,0:T(8,128)S(1)} %bitcast.7), custom_call_target="tpu_custom_call" | custom-call | tf_op jit(solution)/shard_map/collect/pallas_call | solution.py:373
  (13 shorter events, 0.1 us)
Async XLA Ops:
  0.0 12.0 %copy-start = (bf16[128,4096]{1,0:T(8,128)(2,1)S(1)}, bf16[128,4096]{1,0:T(8,128)(2,1)}, u32[]{:S(2)}) copy-start(bf16[128,4096]{1,0:T(8,128)(2,1)} %p_ref.1) | copy-start | bytes 3145732
  4.4 1.2 %copy-start.1 = (bf16[1,8,4,128,128]{4,3,2,1,0:T(8,128)(2,1)S(1)}, bf16[1,8,4,128,128]{4,3,2,1,0:T(8,128)(2,1)}, u32[]{:S(2)}) copy-start(bf16[1,8,4,128,128]{4,3,2,1,0:T(8,128)(2,1)} %param.7) | copy-start | bytes 3145732

commit v4 on v3

--- a/solution.py
+++ b/solution.py
@@ -10,6 +10,8 @@
 MESH = pl.DeviceIdType.MESH
 PIECES = 4
 LOCAL = 2
+AHEAD = 2
+LEND_AT = 0
 
 
 def turn_kernel(n, w_ref, pat_ref, wt_ref, pg_ref, send_sem, recv_sem):
@@ -211,12 +213,8 @@
                 total = runs[code >> 1]
                 target[at, peer, slot] = jnp.where((code & 1) == 1, total, jnp.zeros_like(total))
 
-    for c in range(LOCAL):
+    for c in range(AHEAD):
         start_own(c)
-
-    @pl.when(is_end)
-    def _():
-        lend().start()
 
     def piece(c, carry):
         at_home = jnp.logical_not(is_end) | (c < LOCAL)
@@ -235,9 +233,14 @@
                     def _():
                         send(way, hop + 1, c).start()
             if hop == 0:
-                @pl.when(c + LOCAL < pieces)
+                @pl.when(c + AHEAD < pieces)
                 def _():
-                    start_own(c + LOCAL)
+                    start_own(c + AHEAD)
+
+                @pl.when(is_end & (c == LEND_AT))
+                def _():
+                    lend().start()
+
             for way in range(2):
                 @pl.when(lands(way, hop, c))
                 def _():
@@ -365,7 +368,7 @@
         out_ref[dest_ref[e]] += in_ref[e].T
         return carry
 
-    lax.fori_loop(0, count, step, 0)
+    lax.fori_loop(0, count, step, 0, unroll=4)
 
 
 def collect(dest, received, capacity):

time: 98.3 us -> 91.1 us (0.927)
  Pallas kernels: 91.5 us -> 84.3 us
    pallas_call x1, Pallas kernels: 80.7 us -> 75.6 us  [fused(): pl.pallas_call(functools.partial(fused_kernel, n, owners), out_shape=jax....]
    pallas_call x1, Pallas kernels: 5.33 us -> 3.24 us  [collect(): pl.pallas_call(functools.partial(collect_kernel, count), out_shape=jax.Sh...]
where the time goes in v4:
time: 91.1 us; the launch traced here: 90.8 us
  Pallas kernels  84.3 us (93%)
  local copies, waits for them, and re-layouts  4.21 us (5%)
  other arithmetic  2.17 us (2%)
    pallas_call x1, Pallas kernels, fused(): pl.pallas_call(functools.partial(fused_kernel, n, owners), out_shape=jax....  75.6 us
    pallas_call x1, Pallas kernels, turn(): pl.pallas_call(functools.partial(turn_kernel, n), out_shape=(jax.ShapeDty...  5.54 us
    pallas_call x1, Pallas kernels, collect(): pl.pallas_call(functools.partial(collect_kernel, count), out_shape=jax.Sh...  3.24 us
    unnamed x5, local copies, waits for them, and re-layouts  1.98 us

profile of v4, /device:TPU:1, one launch (start us, length us, event | category | flops | bytes accessed | tf_op | source)
XLA Modules:
  0.0 90.8 jit_solution(17612256159190649589)
XLA Ops:
  0.0 0.0 copy-start
  0.0 0.9 eq.32
  0.9 0.8 copy.10
  1.6 0.1 reshape_squeeze.3
  1.7 0.8 fusion.3
  2.5 0.1 eq.34
  2.6 0.1 select_reduce_fusion
  2.7 0.1 ne.56
  2.8 0.1 div.21
  2.9 0.1 rem.33
  3.0 0.3 convert_reduce_fusion
  3.3 0.2 select_reduce_fusion.2
  3.5 0.7 gather_fusion
  4.2 0.1 copy.9
  4.3 0.1 reshape.135.dest_ref
  4.4 0.0 copy-start.1
  4.4 1.2 %copy-done.1 = bf16[1,8,4,128,128]{4,3,2,1,0:T(8,128)(2,1)S(1)} copy-done((bf16[1,8,4,128,128]{4,3,2,1,0:T(8,128)(2,1)S(1)}, bf16[1,8,4,128,128]{4,3,2,1,0:T(8,128)(2,1)}, u32[]{:S(2)}) %copy-start.1) | copy-done | bytes 1048600
  5.6 5.5 %turn_weights.1 = (bf16[4,8,4,32,128]{4,3,2,1,0:T(8,128)(2,1)S(1)}, s32[4,8,128]{2,1,0:T(8,128)S(1)}) custom-call(bf16[8,4,128,128]{3,2,1,0:T(8,128)(2,1)S(1)} %bitcast.8, s32[8,128]{1,0:T(8,128)S(1)} %pad.4.pat_ref), custom_call_target="tpu_custom_call" | custom-call | tf_op jit(solution)/shard_map/turn_weights/pallas_call | solution.py:58
  11.2 0.1 lt.89
  11.3 0.1 fusion.2
  11.4 0.1 convert_reduce_fusion.2
  11.5 0.2 fusion.1
  11.7 0.2 convert_reduce_fusion.1
  11.9 0.1 select_reduce_fusion.1.hit_ref
  12.0 0.0 copy-done
  12.0 75.6 %gather_multiply_exchange.1 = f32[8,4,4,32,128]{4,3,2,1,0:T(8,128)S(1)} custom-call(s32[128]{0:T(128)S(1)} %select_reduce_fusion.1.hit_ref, s32[32]{0:T(128)S(1)} %convert_add_fusion.last_ref, bf16[4,8,4,32,128]{4,3,2,1,0:T(8,128)(2,1)S(1)} %get-tuple-element.8.w_ref, bf16[128,4096]{1,0:T(8,128)(2,1)S(1)} %copy-done), custom_call_target="tpu_custom_call" | custom-call | tf_op jit(solution)/shard_map/gather_multiply_exchange/pallas_call | solution.py:320
  87.6 3.2 %collect.1 = f32[36,128,128]{2,1,0:T(8,128)} custom-call(s32[32]{0:T(128)S(1)} %reshape.135.dest_ref, f32[32,128,128]{2,1,0:T(8,128)S(1)} %bitcast.7), custom_call_target="tpu_custom_call" | custom-call | tf_op jit(solution)/shard_map/collect/pallas_call | solution.py:376
  (13 shorter events, 0.1 us)
Async XLA Ops:
  0.0 12.0 %copy-start = (bf16[128,4096]{1,0:T(8,128)(2,1)S(1)}, bf16[128,4096]{1,0:T(8,128)(2,1)}, u32[]{:S(2)}) copy-start(bf16[128,4096]{1,0:T(8,128)(2,1)} %p_ref.1) | copy-start | bytes 3145732
  4.4 1.2 %copy-start.1 = (bf16[1,8,4,128,128]{4,3,2,1,0:T(8,128)(2,1)S(1)}, bf16[1,8,4,128,128]{4,3,2,1,0:T(8,128)(2,1)}, u32[]{:S(2)}) copy-start(bf16[1,8,4,128,128]{4,3,2,1,0:T(8,128)(2,1)} %param.7) | copy-start | bytes 3145732
